TPU v7x, 512 devices: a whole 4x4x16 slice. The times are simulated.
512 devices in a mesh: row: 32 (over z, y_hi), col: 16 (over y_lo, x, core).
Axes of the slice: x: 4, y: 4 (y_hi: 2, y_lo: 2; y = y_hi * 2 + y_lo), z: 16, core: 2. Of those that a mesh axis runs over, the one named last changes fastest.
Arguments:
- doc_feats: float32 [1024, 16384], P('row', 'col'), may hold values from -6 to 6
- kernel_inv: float32 [16384, 16384], P('row', 'col'), may hold values from -0.046875 to 0.046875
- target_feats: float32 [256, 16384], P('row'), may hold values from -0.046875 to 0.046875
- doc_weight: float32 [1024], P('row'), may hold values from 0.1 to 1
Outputs:
- scores: float32 [1024, 256], P(('row', 'col'))
All inputs are finite; a program needn't handle non-finite values.
Results may differ from a plain program's by a relative error of at most 0.000094.
Values sent between devices are 32-bit elements; how exact they have to be, the bound alone decides.
No kernel may reach another device: no remote copies, remote signals or barrier semaphores. Data moves between devices by JAX's collectives and lax.ppermute only.
A program may use at most 64 MiB of HBM per device.

v0:
```python
import jax
import jax.numpy as jnp
from jax import lax
from jax.sharding import PartitionSpec as P


def contract_last(left, right):
    return lax.dot_general(
        left,
        right,
        (((1,), (1,)), ((), ())),
        precision=lax.Precision.HIGHEST,
        preferred_element_type=jnp.float32,
    )


def on_device(doc_feats, kernel_inv, target_feats, doc_weight):
    targets_split = lax.all_to_all(target_feats, "row", split_axis=1, concat_axis=0, tiled=True)
    partial_rows = contract_last(lax.all_gather(doc_feats, "row", axis=0, tiled=True), kernel_inv)
    weighted = lax.psum_scatter(partial_rows, "col", scatter_dimension=1, tiled=True)
    width = weighted.shape[1]
    own_cols = lax.dynamic_slice_in_dim(targets_split, lax.axis_index("col") * width, width, 1)
    terms = contract_last(weighted, own_cols)
    scores = lax.psum_scatter(terms, ("row", "col"), scatter_dimension=0, tiled=True)
    count = scores.shape[0]
    own_weight = lax.dynamic_slice_in_dim(doc_weight, lax.axis_index("col") * count, count, 0)
    return scores * own_weight[:, None]


def solution(mesh):
    in_specs = (P("row", "col"), P("row", "col"), P("row", None), P("row"))
    out_specs = P(("row", "col"), None)
    return jax.shard_map(
        on_device, mesh=mesh, in_specs=in_specs, out_specs=out_specs, check_vma=False
    )
```

profile of v0, /device:TPU:1, one launch (start us, length us, event | category | flops | bytes accessed | tf_op | source)
XLA Modules:
  0.0 734.8 jit_solution(12698291684557621382)
XLA Ops:
  6.5 0.0 copy-start
  6.5 0.0 all-gather.2.cloned.1.call-start
  6.5 0.7 all-gather.2.cloned.1.call-update
  7.3 0.0 reduce-scatter.4.cloned.1.call-start
  7.3 164.5 %all-gather.2.cloned.1.call-done = f32[1024,1024]{1,0:T(8,128)} async-done(((f32[32,1024]{1,0:T(8,128)}), f32[1024,1024]{1,0:T(8,128)}) %all-gather.2.cloned.1.call-update) | async-done | bytes 4194320 | tf_op jit(solution)/shard_map/all_gather | solution.py:19
  171.8 0.0 copy-done
  171.8 9.6 %convolution_bitcast_fusion = f32[512,1024]{1,0:T(8,128)} fusion(f32[1024,1024]{1,0:T(8,128)} %all-gather.2.cloned.1.call-done, f32[512,1024]{1,0:T(8,128)S(1)} %copy-done), kind=kOutput, calls=%fused_computation | convolution fusion | flops 6442450944 | bytes 8388608
  181.4 0.0 reduce-scatter.4.cloned.1.call-update
  181.4 0.0 copy-start.1
  181.4 6.9 all-to-all-start
  188.4 0.0 all-reduce.3.cloned.1.call-start
  188.4 23.2 %all-to-all-done = f32[8,32,512]{2,0,1:T(8,128)S(1)} async-done(((f32[8,32,512]{2,0,1:T(8,128)}), f32[8,32,512]{2,0,1:T(8,128)S(1)}, u32[]{:S(2)}, u32[]{:S(2)}) %all-to-all-start) | async-done | bytes 524320 | tf_op jit(solution)/shard_map/all_to_all | solution.py:18
  211.7 41.8 %reduce-scatter.4.cloned.1.call-done = f32[32,1024]{1,0:T(8,128)} async-done(((f32[512,1024]{1,0:T(8,128)}), f32[32,1024]{1,0:T(8,128)}) %reduce-scatter.4.cloned.1.call-update) | async-done | bytes 131088
  253.5 3.0 fusion
  256.4 0.0 all-reduce.3.cloned.1.call-update
  256.4 0.0 copy-done.1
  256.4 0.1 dynamic_slice.7
  256.5 470.4 %all-reduce.3.cloned.1.call-done = f32[1024,256]{1,0:T(8,128)} async-done(((f32[1024,256]{1,0:T(8,128)}), f32[1024,256]{1,0:T(8,128)}) %all-reduce.3.cloned.1.call-update) | async-done | bytes 1048592
  727.0 1.3 dynamic-slice_multiply_fusion
Async XLA Ops:
  6.5 165.3 %copy-start = (f32[512,1024]{1,0:T(8,128)S(1)}, f32[512,1024]{1,0:T(8,128)}, u32[]{:S(2)}) copy-start(f32[512,1024]{1,0:T(8,128)} %param.5) | copy-start | bytes 6291460
  6.5 165.3 %all-gather.2.cloned.1.call-start = ((), (), s32[]{:S(2)}) async-start(), calls=%async_computation.2 | async-start | bytes 4325376 | tf_op jit(solution)/shard_map/all_gather | solution.py:19
  7.3 246.2 %reduce-scatter.4.cloned.1.call-start = ((), (), s32[]{:S(2)}) async-start(), calls=%async_computation.3 | async-start | bytes 2228224
  181.4 75.0 %copy-start.1 = (f32[32]{0:T(128)S(1)}, f32[32]{0:T(128)}, u32[]{:S(2)}) copy-start(f32[32]{0:T(128)} %param.7) | copy-start | bytes 388
  181.4 30.2 %all-to-all-start = ((f32[8,32,512]{2,0,1:T(8,128)}), f32[8,32,512]{2,0,1:T(8,128)S(1)}, u32[]{:S(2)}, u32[]{:S(2)}) async-start(f32[8,32,512]{2,0,1:T(8,128)} %bitcast), calls=%async_computation | async-start | bytes 1048576 | tf_op jit(solution)/shard_map/all_to_all | solution.py:18
  188.4 538.6 %all-reduce.3.cloned.1.call-start = ((), (), s32[]{:S(2)}) async-start(), calls=%async_computation.4 | async-start | bytes 2097152
Sparse Core Ops, SparseCore 0:
  10.5 161.3 all-gather.1
  181.6 71.8 reduce-scatter.3
  258.9 467.9 all-reduce.2
where the time goes:
time: 735 us
  waiting for transfers between devices  701 us (95%)
  between operations  13.1 us (2%)
  matrix products  12.5 us (2%)
    unnamed x5, waiting for transfers between devices  513 us
    all_gather x1, waiting for transfers between devices, on_device(): lax.all_gather(doc_feats, 'row', axis=0, tiled=True)  165 us
    all_to_all x1, waiting for transfers between devices, on_device(): lax.all_to_all(target_feats, 'row', split_axis=1, concat_axis=0, tiled=True)  23.2 us
  transfers between devices with their start and end apart: 4, of which 4 were waited for; matrix products, arithmetic and copies ran while one was open for 0% of the time, Pallas kernels for 0%

commit v1 on v0

v1 whole, which is shorter than its diff:
```python
import functools

import jax
import jax.numpy as jnp
from jax import lax
from jax.experimental import pallas as pl
from jax.experimental.pallas import tpu as pltpu
from jax.sharding import Mesh, PartitionSpec as P

NEAR = 4
VMEM = pl.BlockSpec(memory_space=pltpu.VMEM)
SMEM = pl.BlockSpec(memory_space=pltpu.SMEM)
PARAMS = pltpu.CompilerParams(vmem_limit_bytes=24 * 2**20)


def exchange(pieces, axis):
    return lax.all_to_all(pieces, axis, split_axis=0, concat_axis=0, tiled=True)


def split(x):
    hi = x.astype(jnp.bfloat16)
    return hi, (x - hi.astype(jnp.float32)).astype(jnp.bfloat16)


def dot3(left, right, left_dim, right_dim):
    def one(a, b):
        return lax.dot_general(
            a, b, (((left_dim,), (right_dim,)), ((), ())), preferred_element_type=jnp.float32
        )

    return one(left[0], right[0]) + (one(left[0], right[1]) + one(left[1], right[0]))


def cost(flops, size):
    return pl.CostEstimate(flops=flops, bytes_accessed=size, transcendentals=0)


def split_inverse(kernel_inv):
    n_i, n_j = kernel_inv.shape
    steps = 4

    def body(k_ref, hi_ref, lo_ref):
        hi_ref[...], lo_ref[...] = split(k_ref[...])

    block = pl.BlockSpec((n_i // steps, n_j), lambda s: (s, 0))
    half = jax.ShapeDtypeStruct((n_i, n_j), jnp.bfloat16)
    return pl.pallas_call(
        body,
        grid=(steps,),
        in_specs=[block],
        out_specs=[block, block],
        out_shape=[half, half],
        compiler_params=PARAMS,
        cost_estimate=cost(n_i * n_j * 4, n_i * n_j * 8),
        name="split_inverse",
    )(kernel_inv)


def mix_targets(core, mine, other, k_hi, k_lo):
    all_t, half = mine.shape
    n_j = k_hi.shape[1]
    sub = n_j // NEAR

    def body(core_ref, mine_ref, other_ref, hi_ref, lo_ref, out_ref):
        place = core_ref[0]
        sides = [(split(mine_ref[...]), place), (split(other_ref[...]), 1 - place)]
        for a in range(NEAR):
            cut = slice(a * sub, (a + 1) * sub)
            total = None
            for t, at in sides:
                rows = pl.ds(pl.multiple_of(at * half, half), half)
                part = dot3(t, (hi_ref[rows, cut], lo_ref[rows, cut]), 1, 0)
                total = part if total is None else total + part
            out_ref[a] = total

    return pl.pallas_call(
        body,
        in_specs=[SMEM, VMEM, VMEM, VMEM, VMEM],
        out_specs=VMEM,
        out_shape=jax.ShapeDtypeStruct((NEAR, all_t, sub), jnp.float32),
        compiler_params=PARAMS,
        cost_estimate=cost(6 * all_t * 2 * half * n_j, 4 * 2**20),
        name="mix_targets",
    )(core, mine, other, k_hi, k_lo)


def split_docs(docs, far, chips):
    n, width = docs.shape
    group = n // far // chips

    def body(x_ref, hi_ref, lo_ref):
        x = x_ref[...].reshape(far * group, width)
        hi_ref[...], lo_ref[...] = split(x)

    out = pl.BlockSpec((far * group, width), lambda s: (s, 0))
    half = jax.ShapeDtypeStruct((n, width), jnp.bfloat16)
    return pl.pallas_call(
        body,
        grid=(chips,),
        in_specs=[pl.BlockSpec((far, None, group, width), lambda s: (0, s, 0, 0))],
        out_specs=[out, out],
        out_shape=[half, half],
        compiler_params=PARAMS,
        cost_estimate=cost(2**38, 4 * n * width),
        name="split_docs",
    )(docs.reshape(far, chips, group, width))


def score_docs(d_hi, d_lo, mixed, pair):
    n, width = d_hi.shape
    all_t, sub = mixed.shape

    def body(hi_ref, lo_ref, mixed_ref, pair_ref, out_ref):
        near = dot3((hi_ref[:, :sub], lo_ref[:, :sub]), split(mixed_ref[...]), 1, 1)
        out_ref[...] = near + dot3((hi_ref[:, sub:], lo_ref[:, sub:]), split(pair_ref[...]), 1, 1)

    return pl.pallas_call(
        body,
        in_specs=[VMEM] * 4,
        out_specs=VMEM,
        out_shape=jax.ShapeDtypeStruct((n, all_t), jnp.float32),
        compiler_params=PARAMS,
        cost_estimate=cost(6 * n * width * all_t, 2 * 2**20),
        name="score_docs",
    )(d_hi, d_lo, mixed, pair)


def solution(mesh):
    rows, cols = mesh.shape["row"], mesh.shape["col"]
    far, chips = rows // NEAR, cols // 2
    names = ("far", "near", "chip", "core")
    fine = Mesh(mesh.devices.reshape(far, NEAR, chips, 2), names)
    row, col = ("far", "near"), ("chip", "core")
    swap = [(0, 1), (1, 0)]

    def on_device(doc_feats, kernel_inv, target_feats, doc_weight):
        core = lax.axis_index("core")
        n_t, p = target_feats.shape
        n_i, n_j = kernel_inv.shape
        n_d = doc_feats.shape[0]
        half, sub, own = n_i // 2, n_j // NEAR, n_d // cols
        all_t = rows * n_t

        docs = doc_feats.reshape(chips, 2, own, NEAR, sub).transpose(3, 1, 0, 2, 4)
        docs = exchange(docs.reshape(NEAR * 2, chips * own, sub), ("near", "core"))
        docs = docs.reshape(NEAR, 2, chips, own, sub)
        docs = jnp.where(core == 0, docs, docs[:, ::-1])
        docs = docs.transpose(2, 0, 3, 1, 4).reshape(chips * NEAR * own, 2 * sub)

        cut = target_feats.reshape(n_t, rows, 2, half)
        cut = lax.dynamic_index_in_dim(cut, core, 2, keepdims=False).transpose(1, 0, 2)
        docs, cut = lax.optimization_barrier((docs, cut))
        docs = lax.all_gather(docs, "far", axis=0, tiled=True)
        d_hi, d_lo = split_docs(docs, far, chips)

        k_hi, k_lo = split_inverse(kernel_inv)
        mine = exchange(cut, row).reshape(all_t, half)
        other = lax.ppermute(mine, "core", swap)
        mixed = mix_targets(core.reshape(1), mine, other, k_hi, k_lo)
        mixed = exchange(mixed, "near").sum(0)
        mixed, d_hi, d_lo = lax.optimization_barrier((mixed, d_hi, d_lo))
        pair = lax.ppermute(mixed, "core", swap)

        terms = score_docs(d_hi, d_lo, mixed, pair)
        terms = exchange(terms.reshape(chips, rows * own, all_t), "chip").sum(0)
        scores = exchange(terms.reshape(rows, own, all_t), row).sum(0)
        place = lax.axis_index("chip") * 2 + core
        own_weight = lax.dynamic_slice_in_dim(doc_weight, place * own, own, 0)
        return scores * own_weight[:, None]

    in_specs = (P(row, col), P(row, col), P(row, None), P(row))
    return jax.shard_map(
        on_device, mesh=fine, in_specs=in_specs, out_specs=P(row + col, None), check_vma=False
    )
```

time: 735 us -> 142 us (0.19)
  waiting for transfers between devices: 701 us -> 37 us
  blocking collectives: 0 us -> 48.4 us
  starting transfers between devices: 7.01 us -> 31.4 us
  matrix products: 12.5 us -> 0 us
    unnamed x5 -> x1, waiting for transfers between devices: 513 us -> 0.02 us
    all_gather x1, waiting for transfers between devices: 165 us -> 8.67 us  [on_device(): docs = lax.all_gather(docs, 'far', axis=0, tiled=True)]
    all_to_all x0 -> x2, blocking collectives: none -> 48.4 us  [exchange(): return lax.all_to_all(pieces, axis, split_axis=0, concat_axis=0, tiled=True)]
    all_to_all x1 -> x3, starting transfers between devices: 6.93 us -> 23.6 us  [exchange(): return lax.all_to_all(pieces, axis, split_axis=0, concat_axis=0, tiled=True)]
    unnamed x1 -> x0, matrix products: 9.58 us -> none
    ppermute x0 -> x2, starting transfers between devices: none -> 7.84 us  [the longest x1 5.48 us: on_device(): other = lax.ppermute(mine, 'core', swap)]
    all_to_all x1 -> x3, waiting for transfers between devices: 23.2 us -> 26.5 us  [exchange(): return lax.all_to_all(pieces, axis, split_axis=0, concat_axis=0, tiled=True)]
  transfers between devices with their start and end apart: 4 -> 6, of which waited for: 4 -> 6; matrix products, arithmetic and copies ran while one was open for 0% -> 0% of each run, Pallas kernels for 0% -> 2%
where the time goes in v1:
time: 142 us; the launch traced here: 141 us
  blocking collectives  48.4 us (34%)
  waiting for transfers between devices  37 us (26%)
  starting transfers between devices  31.4 us (22%)
  between operations  13.5 us (10%)
  local copies, waits for them, and re-layouts  4.76 us (3%)
  Pallas kernels  3.35 us (2%)
  other arithmetic  2.1 us (1%)
    all_to_all x2, blocking collectives, exchange(): return lax.all_to_all(pieces, axis, split_axis=0, concat_axis=0, tiled=True)  48.4 us
    all_to_all x3, waiting for transfers between devices, exchange(): return lax.all_to_all(pieces, axis, split_axis=0, concat_axis=0, tiled=True)  26.5 us
    all_to_all x3, starting transfers between devices, exchange(): return lax.all_to_all(pieces, axis, split_axis=0, concat_axis=0, tiled=True)  23.6 us
    all_gather x1, waiting for transfers between devices, on_device(): docs = lax.all_gather(docs, 'far', axis=0, tiled=True)  8.67 us
    ppermute x1, starting transfers between devices, on_device(): other = lax.ppermute(mine, 'core', swap)  5.48 us
  transfers between devices with their start and end apart: 6, of which 6 were waited for; matrix products, arithmetic and copies ran while one was open for 0% of the time, Pallas kernels for 2%

profile of v1, /device:TPU:1, one launch (start us, length us, event | category | flops | bytes accessed | tf_op | source)
XLA Modules:
  0.0 140.5 jit_solution(16820221476746689703)
XLA Ops:
  6.5 0.0 copy-start
  6.5 0.0 copy-start.1
  6.5 1.1 reshape.32
  7.7 0.1 copy.16
  7.7 0.7 reshape.33
  8.5 10.1 %all-to-all-start = ((f32[8,16,256]{2,1,0:T(8,128)}), f32[8,16,256]{2,1,0:T(8,128)S(1)}, u32[]{:S(2)}, u32[]{:S(2)}) async-start(f32[8,16,256]{2,1,0:T(8,128)} %reshape.33), calls=%async_computation | async-start | bytes 262144 | tf_op jit(solution)/shard_map/all_to_all | solution.py:17
  18.6 0.0 all-gather.2.cloned.1.call-start
  18.6 0.0 copy-done
  18.7 5.8 %all-to-all-done = f32[8,16,256]{2,1,0:T(8,128)S(1)} async-done(((f32[8,16,256]{2,1,0:T(8,128)}), f32[8,16,256]{2,1,0:T(8,128)S(1)}, u32[]{:S(2)}, u32[]{:S(2)}) %all-to-all-start) | async-done | bytes 131104 | tf_op jit(solution)/shard_map/all_to_all | solution.py:17
  24.4 0.1 reshape.34
  24.6 0.1 copy.11
  24.7 0.7 copy.14
  25.3 0.0 all-gather.2.cloned.1.call-update
  25.3 35.2 %all_to_all.25 = f32[32,8,256]{2,1,0:T(8,128)S(1)} all-to-all(f32[32,8,256]{2,1,0:T(8,128)S(1)} %dynamic-slice_bitcast_fusion), channel_id=1, replica_groups=mesh['far'=8,'near'=4,'chip'=8,'core'=2] {'far','near'}, dimensions={0} | all-to-all | bytes 524288 | tf_op jit(solution)/shard_map/all_to_all | solution.py:17
  60.6 5.5 %collective-permute-start = (f32[256,256]{1,0:T(8,128)S(1)}, f32[256,256]{1,0:T(8,128)S(1)}, u32[]{:S(2)}, u32[]{:S(2)}) collective-permute-start(f32[256,256]{1,0:T(8,128)S(1)} %bitcast.19), channel_id=1, source_target_pairs={{0,1},{1,0},{2,3},{3,2},{4,5},{5,4},{6,7},{7,6},{8,9},{9,8},{10,11... | collective-permute-start | bytes 786440 | tf_op jit(solution)/shard_map/ppermute | solution.py:158
  66.1 0.0 copy-done.1
  66.1 0.4 split_inverse.1
  66.5 0.7 collective-permute-done.other_ref
  67.2 2.0 %mix_targets.1 = f32[4,256,256]{2,1,0:T(8,128)} custom-call(s32[1]{0:T(128)} %bitcast.core_ref, f32[256,256]{1,0:T(8,128)S(1)} %bitcast.20, f32[256,256]{1,0:T(8,128)S(1)} %collective-permute-done.other_ref, bf16[512,1024]{1,0:T(8,128)(2,1)S(1)} %get-tuple-element.15.hi_ref, bf16[512,1024]{1,0:T(8,128)(2,1)S(1)} %get-tuple-element.16.lo_ref), custom_call_target="tpu_custom_call" | custom-call | flops 805306368 | bytes 4194304 | tf_op jit(solution)/shard_map/mix_targets/pallas_call | solution.py:76
  69.2 4.7 %all-to-all-start.2 = ((f32[4,256,256]{2,1,0:T(8,128)}), f32[4,256,256]{2,1,0:T(8,128)}, u32[]{:S(2)}, u32[]{:S(2)}) async-start(f32[4,256,256]{2,1,0:T(8,128)} %mix_targets.1), calls=%async_computation.2 | async-start | bytes 2097152 | tf_op jit(solution)/shard_map/all_to_all | solution.py:17
  73.9 8.7 %all-gather.2.cloned.1.call-done = f32[512,512]{1,0:T(8,128)} async-done(((f32[64,512]{1,0:T(8,128)}), f32[512,512]{1,0:T(8,128)}) %all-gather.2.cloned.1.call-update) | async-done | bytes 1048592 | tf_op jit(solution)/shard_map/all_gather | solution.py:153
  82.6 0.0 copy-start.2
  82.6 1.2 copy-done.2
  83.8 0.3 split_docs.1
  84.2 6.7 %all-to-all-done.2 = f32[4,256,256]{2,1,0:T(8,128)} async-done(((f32[4,256,256]{2,1,0:T(8,128)}), f32[4,256,256]{2,1,0:T(8,128)}, u32[]{:S(2)}, u32[]{:S(2)}) %all-to-all-start.2) | async-done | bytes 1048608 | tf_op jit(solution)/shard_map/all_to_all | solution.py:17
  90.9 1.3 reduce_sum.27.mixed_ref
  92.2 0.0 copy-start.3
  92.2 2.4 %collective-permute-start.1 = (f32[256,256]{1,0:T(8,128)S(1)}, f32[256,256]{1,0:T(8,128)S(1)}, u32[]{:S(2)}, u32[]{:S(2)}) collective-permute-start(f32[256,256]{1,0:T(8,128)S(1)} %reduce_sum.27.mixed_ref), channel_id=1, source_target_pairs={{0,1},{1,0},{2,3},{3,2},{4,5},{5,4},{6,7},{7,6},{8,9},{9,8},{10,11... | collective-permute-start | bytes 786440 | tf_op jit(solution)/shard_map/ppermute | solution.py:162
  94.6 1.1 collective-permute-done.1.pair_ref
  95.7 0.6 score_docs.1
  96.3 13.1 %all_to_all.26 = f32[8,64,256]{2,1,0:T(8,128)S(1)} all-to-all(f32[8,64,256]{2,1,0:T(8,128)S(1)} %bitcast.18), channel_id=1, replica_groups=mesh['far'=8,'near'=4,'chip'=8,'core'=2] {'chip'}, dimensions={0} | all-to-all | bytes 1048576 | tf_op jit(solution)/shard_map/all_to_all | solution.py:17
  109.5 0.7 reshape.40
  110.2 8.7 %all-to-all-start.4 = ((f32[32,2,256]{2,1,0:T(2,128)}), f32[32,2,256]{2,1,0:T(2,128)S(1)}, u32[]{:S(2)}, u32[]{:S(2)}) async-start(f32[32,2,256]{2,1,0:T(2,128)} %reshape.40), calls=%async_computation.4 | async-start | bytes 131072 | tf_op jit(solution)/shard_map/all_to_all | solution.py:17
  118.8 0.0 copy-done.3
  118.9 0.1 dynamic_slice.8
  118.9 14.1 %all-to-all-done.4 = f32[32,2,256]{2,1,0:T(2,128)S(1)} async-done(((f32[32,2,256]{2,1,0:T(2,128)}), f32[32,2,256]{2,1,0:T(2,128)S(1)}, u32[]{:S(2)}, u32[]{:S(2)}) %all-to-all-start.4) | async-done | bytes 65568 | tf_op jit(solution)/shard_map/all_to_all | solution.py:17
  133.0 0.6 broadcast_multiply_fusion
  (4 shorter events, 0.2 us)
Async XLA Ops:
  6.5 12.1 %copy-start = (f32[8,16384]{1,0:T(8,128)S(1)}, f32[8,16384]{1,0:T(8,128)}, u32[]{:S(2)}) copy-start(f32[8,16384]{1,0:T(8,128)} %param.6) | copy-start | bytes 1572868
  6.5 59.5 %copy-start.1 = (f32[512,1024]{1,0:T(8,128)S(1)}, f32[512,1024]{1,0:T(8,128)}, u32[]{:S(2)}) copy-start(f32[512,1024]{1,0:T(8,128)} %k_ref.1) | copy-start | bytes 6291460
  8.5 16.0 %all-to-all-start = ((f32[8,16,256]{2,1,0:T(8,128)}), f32[8,16,256]{2,1,0:T(8,128)S(1)}, u32[]{:S(2)}, u32[]{:S(2)}) async-start(f32[8,16,256]{2,1,0:T(8,128)} %reshape.33), calls=%async_computation | async-start | bytes 262144 | tf_op jit(solution)/shard_map/all_to_all | solution.py:17
  18.6 64.0 %all-gather.2.cloned.1.call-start = ((), (), s32[]{:S(2)}) async-start(), calls=%async_computation.5 | async-start | bytes 1179648 | tf_op jit(solution)/shard_map/all_gather | solution.py:153
  60.6 6.6 %collective-permute-start = (f32[256,256]{1,0:T(8,128)S(1)}, f32[256,256]{1,0:T(8,128)S(1)}, u32[]{:S(2)}, u32[]{:S(2)}) collective-permute-start(f32[256,256]{1,0:T(8,128)S(1)} %bitcast.19), channel_id=1, source_target_pairs={{0,1},{1,0},{2,3},{3,2},{4,5},{5,4},{6,7},{7,6},{8,9},{9,8},{10,11... | collective-permute-start | bytes 786440 | tf_op jit(solution)/shard_map/ppermute | solution.py:158
  69.2 21.7 %all-to-all-start.2 = ((f32[4,256,256]{2,1,0:T(8,128)}), f32[4,256,256]{2,1,0:T(8,128)}, u32[]{:S(2)}, u32[]{:S(2)}) async-start(f32[4,256,256]{2,1,0:T(8,128)} %mix_targets.1), calls=%async_computation.2 | async-start | bytes 2097152 | tf_op jit(solution)/shard_map/all_to_all | solution.py:17
  82.6 1.2 copy-start.2
  92.2 26.7 %copy-start.3 = (f32[32]{0:T(128)S(1)}, f32[32]{0:T(128)}, u32[]{:S(2)}) copy-start(f32[32]{0:T(128)} %param.7) | copy-start | bytes 388
  92.2 3.5 %collective-permute-start.1 = (f32[256,256]{1,0:T(8,128)S(1)}, f32[256,256]{1,0:T(8,128)S(1)}, u32[]{:S(2)}, u32[]{:S(2)}) collective-permute-start(f32[256,256]{1,0:T(8,128)S(1)} %reduce_sum.27.mixed_ref), channel_id=1, source_target_pairs={{0,1},{1,0},{2,3},{3,2},{4,5},{5,4},{6,7},{7,6},{8,9},{9,8},{10,11... | collective-permute-start | bytes 786440 | tf_op jit(solution)/shard_map/ppermute | solution.py:162
  110.2 22.8 %all-to-all-start.4 = ((f32[32,2,256]{2,1,0:T(2,128)}), f32[32,2,256]{2,1,0:T(2,128)S(1)}, u32[]{:S(2)}, u32[]{:S(2)}) async-start(f32[32,2,256]{2,1,0:T(2,128)} %reshape.40), calls=%async_computation.4 | async-start | bytes 131072 | tf_op jit(solution)/shard_map/all_to_all | solution.py:17
Sparse Core Ops, SparseCore 0:
  25.5 57.0 all-gather.1

commit v2 on v1

--- a/solution.py
+++ b/solution.py
@@ -84,45 +84,73 @@
     )(core, mine, other, k_hi, k_lo)
 
 
-def split_docs(docs, far, chips):
-    n, width = docs.shape
-    group = n // far // chips
-
-    def body(x_ref, hi_ref, lo_ref):
-        x = x_ref[...].reshape(far * group, width)
-        hi_ref[...], lo_ref[...] = split(x)
-
-    out = pl.BlockSpec((far * group, width), lambda s: (s, 0))
+def split_docs(place, blocks, cols):
+    near = len(blocks)
+    each, width = blocks[0].shape
+    own = each // cols
+    group, n = near * own, near * each
+
+    def body(place_ref, *refs):
+        hi_ref, lo_ref, f32_ref = refs[near:]
+        for s in range(near):
+            for k in range(own):
+                at = pl.ds(place_ref[s] * own + k, cols, stride=group)
+                f32_ref[at, :] = refs[s][pl.ds(k, cols, stride=own), :]
+        hi_ref[...], lo_ref[...] = split(f32_ref[...])
+
+    lanes = 128
+    out = pl.BlockSpec((n, lanes), lambda s: (0, s))
     half = jax.ShapeDtypeStruct((n, width), jnp.bfloat16)
     return pl.pallas_call(
         body,
-        grid=(chips,),
-        in_specs=[pl.BlockSpec((far, None, group, width), lambda s: (0, s, 0, 0))],
+        grid=(width // lanes,),
+        in_specs=[SMEM] + [pl.BlockSpec((each, lanes), lambda s: (0, s))] * near,
         out_specs=[out, out],
         out_shape=[half, half],
-        compiler_params=PARAMS,
-        cost_estimate=cost(2**38, 4 * n * width),
+        scratch_shapes=[pltpu.VMEM((n, lanes), jnp.float32)],
+        compiler_params=PARAMS,
+        cost_estimate=cost(4 * n * width, 8 * n * width),
         name="split_docs",
-    )(docs.reshape(far, chips, group, width))
-
-
-def score_docs(d_hi, d_lo, mixed, pair):
+    )(place, *blocks)
+
+
+def sum_copies(parts):
+    n, some_t, sub = parts.shape
+
+    def body(x_ref, out_ref):
+        total = x_ref[0] + x_ref[1]
+        for a in range(2, n):
+            total = total + x_ref[a]
+        for a in range(n):
+            out_ref[a] = total
+
+    return pl.pallas_call(
+        body,
+        in_specs=[VMEM],
+        out_specs=VMEM,
+        out_shape=jax.ShapeDtypeStruct(parts.shape, jnp.float32),
+        compiler_params=PARAMS,
+        cost_estimate=cost(n * some_t * sub, 8 * n * some_t * sub),
+        name="sum_copies",
+    )(parts)
+
+
+def score_docs(d_hi, d_lo, mixed):
     n, width = d_hi.shape
-    all_t, sub = mixed.shape
-
-    def body(hi_ref, lo_ref, mixed_ref, pair_ref, out_ref):
-        near = dot3((hi_ref[:, :sub], lo_ref[:, :sub]), split(mixed_ref[...]), 1, 1)
-        out_ref[...] = near + dot3((hi_ref[:, sub:], lo_ref[:, sub:]), split(pair_ref[...]), 1, 1)
-
-    return pl.pallas_call(
-        body,
-        in_specs=[VMEM] * 4,
+    all_t = mixed.shape[0]
+
+    def body(hi_ref, lo_ref, mixed_ref, out_ref):
+        out_ref[...] = dot3((hi_ref[...], lo_ref[...]), split(mixed_ref[...]), 1, 1)
+
+    return pl.pallas_call(
+        body,
+        in_specs=[VMEM] * 3,
         out_specs=VMEM,
         out_shape=jax.ShapeDtypeStruct((n, all_t), jnp.float32),
         compiler_params=PARAMS,
-        cost_estimate=cost(6 * n * width * all_t, 2 * 2**20),
+        cost_estimate=cost(6 * n * width * all_t, 2**20),
         name="score_docs",
-    )(d_hi, d_lo, mixed, pair)
+    )(d_hi, d_lo, mixed)
 
 
 def solution(mesh):
@@ -141,29 +169,30 @@
         half, sub, own = n_i // 2, n_j // NEAR, n_d // cols
         all_t = rows * n_t
 
-        docs = doc_feats.reshape(chips, 2, own, NEAR, sub).transpose(3, 1, 0, 2, 4)
-        docs = exchange(docs.reshape(NEAR * 2, chips * own, sub), ("near", "core"))
-        docs = docs.reshape(NEAR, 2, chips, own, sub)
-        docs = jnp.where(core == 0, docs, docs[:, ::-1])
-        docs = docs.transpose(2, 0, 3, 1, 4).reshape(chips * NEAR * own, 2 * sub)
-
         cut = target_feats.reshape(n_t, rows, 2, half)
         cut = lax.dynamic_index_in_dim(cut, core, 2, keepdims=False).transpose(1, 0, 2)
-        docs, cut = lax.optimization_barrier((docs, cut))
-        docs = lax.all_gather(docs, "far", axis=0, tiled=True)
-        d_hi, d_lo = split_docs(docs, far, chips)
-
+        mine = exchange(cut, row).reshape(all_t, half)
         k_hi, k_lo = split_inverse(kernel_inv)
-        mine = exchange(cut, row).reshape(all_t, half)
+
+        here = lax.axis_index("near")
+        place = jnp.stack([here ^ s for s in range(NEAR)])
+        blocks = []
+        for s in range(NEAR):
+            block = lax.dynamic_slice_in_dim(doc_feats, place[s] * sub, sub, 1)
+            pairs = [(a, a ^ s) for a in range(NEAR)]
+            blocks.append(lax.ppermute(block, "near", pairs) if s else block)
+        d_hi, d_lo = split_docs(place, blocks, cols)
+        mine, k_hi, k_lo, d_hi, d_lo = lax.optimization_barrier((mine, k_hi, k_lo, d_hi, d_lo))
+
         other = lax.ppermute(mine, "core", swap)
         mixed = mix_targets(core.reshape(1), mine, other, k_hi, k_lo)
         mixed = exchange(mixed, "near").sum(0)
-        mixed, d_hi, d_lo = lax.optimization_barrier((mixed, d_hi, d_lo))
-        pair = lax.ppermute(mixed, "core", swap)
-
-        terms = score_docs(d_hi, d_lo, mixed, pair)
-        terms = exchange(terms.reshape(chips, rows * own, all_t), "chip").sum(0)
-        scores = exchange(terms.reshape(rows, own, all_t), row).sum(0)
+        mixed = exchange(mixed.reshape(far, all_t // far, sub), "far")
+        mixed = exchange(sum_copies(mixed), "far").reshape(all_t, sub)
+
+        terms = score_docs(d_hi, d_lo, mixed)
+        terms = exchange(terms.reshape(cols, NEAR * own, all_t), col).sum(0)
+        scores = exchange(terms.reshape(NEAR, own, all_t), "near").sum(0)
         place = lax.axis_index("chip") * 2 + core
         own_weight = lax.dynamic_slice_in_dim(doc_weight, place * own, own, 0)
         return scores * own_weight[:, None]

time: 142 us -> 137 us (0.965)
  blocking collectives: 48.4 us -> 79 us
  waiting for transfers between devices: 37 us -> 13.3 us
  between operations: 13.5 us -> 0.14 us
  starting transfers between devices: 31.4 us -> 36.1 us
    all_to_all x2 -> x4, blocking collectives: 48.4 us -> 79 us  [exchange(): return lax.all_to_all(pieces, axis, split_axis=0, concat_axis=0, tiled=True)]
    all_to_all x3 -> x2, waiting for transfers between devices: 26.5 us -> 10.9 us  [exchange(): return lax.all_to_all(pieces, axis, split_axis=0, concat_axis=0, tiled=True)]
    all_gather x1 -> x0, waiting for transfers between devices: 8.67 us -> none  [on_device(): docs = lax.all_gather(docs, 'far', axis=0, tiled=True)]
    ppermute x1 -> x3, starting transfers between devices: 2.36 us -> 9.88 us  [on_device(): blocks.append(lax.ppermute(block, 'near', pairs) if s else block)]
    reshape x5 -> x1, local copies, waits for them, and re-layouts: 2.66 us -> 0.6 us  [on_device(): scores = exchange(terms.reshape(NEAR, own, all_t), 'near').sum(0)]
    all_to_all x3 -> x2, starting transfers between devices: 23.6 us -> 21.9 us  [exchange(): return lax.all_to_all(pieces, axis, split_axis=0, concat_axis=0, tiled=True)]
  transfers between devices with their start and end apart: 6 -> 6, of which waited for: 6 -> 5; matrix products, arithmetic and copies ran while one was open for 0% -> 1% of each run, Pallas kernels for 2% -> 1%
where the time goes in v2:
time: 137 us
  blocking collectives  79 us (58%)
  starting transfers between devices  36.1 us (26%)
  waiting for transfers between devices  13.3 us (10%)
  local copies, waits for them, and re-layouts  4.86 us (4%)
  Pallas kernels  2.36 us (2%)
    all_to_all x4, blocking collectives, exchange(): return lax.all_to_all(pieces, axis, split_axis=0, concat_axis=0, tiled=True)  79 us
    all_to_all x2, starting transfers between devices, exchange(): return lax.all_to_all(pieces, axis, split_axis=0, concat_axis=0, tiled=True)  21.9 us
    all_to_all x2, waiting for transfers between devices, exchange(): return lax.all_to_all(pieces, axis, split_axis=0, concat_axis=0, tiled=True)  10.9 us
    ppermute x3, starting transfers between devices, on_device(): blocks.append(lax.ppermute(block, 'near', pairs) if s else block)  9.88 us
    ppermute x1, starting transfers between devices, on_device(): other = lax.ppermute(mine, 'core', swap)  4.31 us
  transfers between devices with their start and end apart: 6, of which 5 were waited for; matrix products, arithmetic and copies ran while one was open for 1% of the time, Pallas kernels for 1%

profile of v2, /device:TPU:1, one launch (start us, length us, event | category | flops | bytes accessed | tf_op | source)
XLA Modules:
  0.0 136.6 jit_solution(2466004778369279465)
XLA Ops:
  0.0 0.0 copy-start
  0.0 1.0 copy-done
  1.0 0.7 dynamic-slice_bitcast_fusion
  1.8 18.7 %all-to-all-start = ((f32[32,8,256]{2,1,0:T(8,128)}), f32[32,8,256]{2,1,0:T(8,128)S(1)}, u32[]{:S(2)}, u32[]{:S(2)}) async-start(f32[32,8,256]{2,1,0:T(8,128)} %dynamic-slice_bitcast_fusion), calls=%async_computation | async-start | bytes 524288 | tf_op jit(solution)/shard_map/all_to_all | solution.py:17
  20.5 0.8 constant_dynamic-slice_fusion
  21.3 5.5 %collective-permute-start.2 = (f32[32,256]{1,0:T(8,128)S(1)}, f32[32,256]{1,0:T(8,128)S(1)}, u32[]{:S(2)}, u32[]{:S(2)}) collective-permute-start(f32[32,256]{1,0:T(8,128)S(1)} %get-tuple-element.23), channel_id=1, source_target_pairs={{0,48},{16,32},{32,16},{48,0},{1,49},{17,33},{33,17},{49,1},{2,50}... | collective-permute-start | bytes 98312 | tf_op jit(solution)/shard_map/ppermute | solution.py:183
  26.8 2.2 %collective-permute-start = (f32[32,256]{1,0:T(8,128)S(1)}, f32[32,256]{1,0:T(8,128)S(1)}, u32[]{:S(2)}, u32[]{:S(2)}) collective-permute-start(f32[32,256]{1,0:T(8,128)S(1)} %get-tuple-element.24), channel_id=1, source_target_pairs={{0,16},{16,0},{32,48},{48,32},{1,17},{17,1},{33,49},{49,33},{2,18}... | collective-permute-start | bytes 98312 | tf_op jit(solution)/shard_map/ppermute | solution.py:183
  29.0 2.1 %collective-permute-start.1 = (f32[32,256]{1,0:T(8,128)S(1)}, f32[32,256]{1,0:T(8,128)S(1)}, u32[]{:S(2)}, u32[]{:S(2)}) collective-permute-start(f32[32,256]{1,0:T(8,128)S(1)} %get-tuple-element.26), channel_id=1, source_target_pairs={{0,32},{16,48},{32,0},{48,16},{1,33},{17,49},{33,1},{49,17},{2,34}... | collective-permute-start | bytes 98312 | tf_op jit(solution)/shard_map/ppermute | solution.py:183
  31.2 0.1 pad_add_fusion.place_ref
  31.3 0.0 copy-start.1
  31.3 1.6 %copy-done.1 = f32[512,1024]{1,0:T(8,128)S(1)} copy-done((f32[512,1024]{1,0:T(8,128)S(1)}, f32[512,1024]{1,0:T(8,128)}, u32[]{:S(2)}) %copy-start.1) | copy-done | bytes 2097176
  32.9 0.4 split_inverse.1
  33.3 0.7 collective-permute-done.2.refs_3_
  34.0 0.0 collective-permute-done.refs_1_
  34.0 0.5 collective-permute-done.1.refs_2_
  34.6 0.7 split_docs.1
  35.2 5.9 %all-to-all-done = f32[32,8,256]{2,1,0:T(8,128)S(1)} async-done(((f32[32,8,256]{2,1,0:T(8,128)}), f32[32,8,256]{2,1,0:T(8,128)S(1)}, u32[]{:S(2)}, u32[]{:S(2)}) %all-to-all-start) | async-done | bytes 262176 | tf_op jit(solution)/shard_map/all_to_all | solution.py:17
  41.2 4.3 %collective-permute-start.3 = (f32[256,256]{1,0:T(8,128)S(1)}, f32[256,256]{1,0:T(8,128)S(1)}, u32[]{:S(2)}, u32[]{:S(2)}) collective-permute-start(f32[256,256]{1,0:T(8,128)S(1)} %bitcast.16), channel_id=1, source_target_pairs={{0,1},{1,0},{2,3},{3,2},{4,5},{5,4},{6,7},{7,6},{8,9},{9,8},{10,11... | collective-permute-start | bytes 786440 | tf_op jit(solution)/shard_map/ppermute | solution.py:187
  45.5 1.1 collective-permute-done.3.other_ref
  46.6 1.0 mix_targets.1
  47.6 18.5 %all_to_all.30 = f32[4,256,256]{2,1,0:T(8,128)S(1)} all-to-all(f32[4,256,256]{2,1,0:T(8,128)S(1)} %mix_targets.1), channel_id=1, replica_groups=mesh['far'=8,'near'=4,'chip'=8,'core'=2] {'near'}, dimensions={0} | all-to-all | bytes 2097152 | tf_op jit(solution)/shard_map/all_to_all | solution.py:17
  66.1 0.0 copy-start.2
  66.1 0.1 reduce_sum.27
  66.2 21.3 %all_to_all.31.x_ref = f32[8,32,256]{2,1,0:T(8,128)S(1)} all-to-all(f32[8,32,256]{2,1,0:T(8,128)S(1)} %bitcast.19), channel_id=1, replica_groups=mesh['far'=8,'near'=4,'chip'=8,'core'=2] {'far'}, dimensions={0} | all-to-all | bytes 524288 | tf_op jit(solution)/shard_map/all_to_all | solution.py:17
  87.5 23.3 %all_to_all.32 = f32[8,32,256]{2,1,0:T(8,128)S(1)} all-to-all(f32[8,32,256]{2,1,0:T(8,128)S(1)} %sum_copies.1), channel_id=1, replica_groups=mesh['far'=8,'near'=4,'chip'=8,'core'=2] {'far'}, dimensions={0} | all-to-all | bytes 524288 | tf_op jit(solution)/shard_map/all_to_all | solution.py:17
  110.8 0.3 score_docs.1
  111.1 15.9 %all_to_all.33 = f32[16,8,256]{2,1,0:T(8,128)S(1)} all-to-all(f32[16,8,256]{2,1,0:T(8,128)S(1)} %bitcast.18), channel_id=1, replica_groups=mesh['far'=8,'near'=4,'chip'=8,'core'=2] {'chip','core'}, dimensions={0} | all-to-all | bytes 262144 | tf_op jit(solution)/shard_map/all_to_all | solution.py:17
  127.0 0.6 reshape.28
  127.7 3.2 %all-to-all-start.5 = ((f32[4,2,256]{2,1,0:T(2,128)}), f32[4,2,256]{2,1,0:T(2,128)S(1)}, u32[]{:S(2)}, u32[]{:S(2)}) async-start(f32[4,2,256]{2,1,0:T(2,128)} %reshape.28), calls=%async_computation.5 | async-start | bytes 16384 | tf_op jit(solution)/shard_map/all_to_all | solution.py:17
  130.9 0.0 copy-done.2
  130.9 0.1 dynamic_slice.24
  131.0 4.9 %all-to-all-done.5 = f32[4,2,256]{2,1,0:T(2,128)S(1)} async-done(((f32[4,2,256]{2,1,0:T(2,128)}), f32[4,2,256]{2,1,0:T(2,128)S(1)}, u32[]{:S(2)}, u32[]{:S(2)}) %all-to-all-start.5) | async-done | bytes 8224 | tf_op jit(solution)/shard_map/all_to_all | solution.py:17
  135.9 0.6 broadcast_multiply_fusion
  (3 shorter events, 0.1 us)
Async XLA Ops:
  0.0 1.0 copy-start
  1.8 39.4 %all-to-all-start = ((f32[32,8,256]{2,1,0:T(8,128)}), f32[32,8,256]{2,1,0:T(8,128)S(1)}, u32[]{:S(2)}, u32[]{:S(2)}) async-start(f32[32,8,256]{2,1,0:T(8,128)} %dynamic-slice_bitcast_fusion), calls=%async_computation | async-start | bytes 524288 | tf_op jit(solution)/shard_map/all_to_all | solution.py:17
  21.3 12.7 %collective-permute-start.2 = (f32[32,256]{1,0:T(8,128)S(1)}, f32[32,256]{1,0:T(8,128)S(1)}, u32[]{:S(2)}, u32[]{:S(2)}) collective-permute-start(f32[32,256]{1,0:T(8,128)S(1)} %get-tuple-element.23), channel_id=1, source_target_pairs={{0,48},{16,32},{32,16},{48,0},{1,49},{17,33},{33,17},{49,1},{2,50}... | collective-permute-start | bytes 98312 | tf_op jit(solution)/shard_map/ppermute | solution.py:183
  26.8 7.2 %collective-permute-start = (f32[32,256]{1,0:T(8,128)S(1)}, f32[32,256]{1,0:T(8,128)S(1)}, u32[]{:S(2)}, u32[]{:S(2)}) collective-permute-start(f32[32,256]{1,0:T(8,128)S(1)} %get-tuple-element.24), channel_id=1, source_target_pairs={{0,16},{16,0},{32,48},{48,32},{1,17},{17,1},{33,49},{49,33},{2,18}... | collective-permute-start | bytes 98312 | tf_op jit(solution)/shard_map/ppermute | solution.py:183
  29.0 5.5 %collective-permute-start.1 = (f32[32,256]{1,0:T(8,128)S(1)}, f32[32,256]{1,0:T(8,128)S(1)}, u32[]{:S(2)}, u32[]{:S(2)}) collective-permute-start(f32[32,256]{1,0:T(8,128)S(1)} %get-tuple-element.26), channel_id=1, source_target_pairs={{0,32},{16,48},{32,0},{48,16},{1,33},{17,49},{33,1},{49,17},{2,34}... | collective-permute-start | bytes 98312 | tf_op jit(solution)/shard_map/ppermute | solution.py:183
  31.3 1.6 %copy-start.1 = (f32[512,1024]{1,0:T(8,128)S(1)}, f32[512,1024]{1,0:T(8,128)}, u32[]{:S(2)}) copy-start(f32[512,1024]{1,0:T(8,128)} %k_ref.1) | copy-start | bytes 6291460
  41.2 5.5 %collective-permute-start.3 = (f32[256,256]{1,0:T(8,128)S(1)}, f32[256,256]{1,0:T(8,128)S(1)}, u32[]{:S(2)}, u32[]{:S(2)}) collective-permute-start(f32[256,256]{1,0:T(8,128)S(1)} %bitcast.16), channel_id=1, source_target_pairs={{0,1},{1,0},{2,3},{3,2},{4,5},{5,4},{6,7},{7,6},{8,9},{9,8},{10,11... | collective-permute-start | bytes 786440 | tf_op jit(solution)/shard_map/ppermute | solution.py:187
  66.1 64.8 %copy-start.2 = (f32[32]{0:T(128)S(1)}, f32[32]{0:T(128)}, u32[]{:S(2)}) copy-start(f32[32]{0:T(128)} %param.7) | copy-start | bytes 388
  127.7 8.3 %all-to-all-start.5 = ((f32[4,2,256]{2,1,0:T(2,128)}), f32[4,2,256]{2,1,0:T(2,128)S(1)}, u32[]{:S(2)}, u32[]{:S(2)}) async-start(f32[4,2,256]{2,1,0:T(2,128)} %reshape.28), calls=%async_computation.5 | async-start | bytes 16384 | tf_op jit(solution)/shard_map/all_to_all | solution.py:17

commit v3 on v2

--- a/solution.py
+++ b/solution.py
@@ -84,32 +84,24 @@
     )(core, mine, other, k_hi, k_lo)
 
 
-def split_docs(place, blocks, cols):
+def split_docs(place, blocks):
     near = len(blocks)
     each, width = blocks[0].shape
-    own = each // cols
-    group, n = near * own, near * each
 
     def body(place_ref, *refs):
-        hi_ref, lo_ref, f32_ref = refs[near:]
+        hi_ref, lo_ref = refs[near:]
         for s in range(near):
-            for k in range(own):
-                at = pl.ds(place_ref[s] * own + k, cols, stride=group)
-                f32_ref[at, :] = refs[s][pl.ds(k, cols, stride=own), :]
-        hi_ref[...], lo_ref[...] = split(f32_ref[...])
+            at = pl.ds(pl.multiple_of(place_ref[s] * each, each), each)
+            hi_ref[at, :], lo_ref[at, :] = split(refs[s][...])
 
-    lanes = 128
-    out = pl.BlockSpec((n, lanes), lambda s: (0, s))
-    half = jax.ShapeDtypeStruct((n, width), jnp.bfloat16)
+    half = jax.ShapeDtypeStruct((near * each, width), jnp.bfloat16)
     return pl.pallas_call(
         body,
-        grid=(width // lanes,),
-        in_specs=[SMEM] + [pl.BlockSpec((each, lanes), lambda s: (0, s))] * near,
-        out_specs=[out, out],
+        in_specs=[SMEM] + [VMEM] * near,
+        out_specs=[VMEM, VMEM],
         out_shape=[half, half],
-        scratch_shapes=[pltpu.VMEM((n, lanes), jnp.float32)],
         compiler_params=PARAMS,
-        cost_estimate=cost(4 * n * width, 8 * n * width),
+        cost_estimate=cost(4 * near * each * width, 8 * near * each * width),
         name="split_docs",
     )(place, *blocks)
 
@@ -181,7 +173,7 @@
             block = lax.dynamic_slice_in_dim(doc_feats, place[s] * sub, sub, 1)
             pairs = [(a, a ^ s) for a in range(NEAR)]
             blocks.append(lax.ppermute(block, "near", pairs) if s else block)
-        d_hi, d_lo = split_docs(place, blocks, cols)
+        d_hi, d_lo = split_docs(place, blocks)
         mine, k_hi, k_lo, d_hi, d_lo = lax.optimization_barrier((mine, k_hi, k_lo, d_hi, d_lo))
 
         other = lax.ppermute(mine, "core", swap)
@@ -191,8 +183,8 @@
         mixed = exchange(sum_copies(mixed), "far").reshape(all_t, sub)
 
         terms = score_docs(d_hi, d_lo, mixed)
-        terms = exchange(terms.reshape(cols, NEAR * own, all_t), col).sum(0)
-        scores = exchange(terms.reshape(NEAR, own, all_t), "near").sum(0)
+        terms = terms.reshape(NEAR * cols, own, all_t)
+        scores = exchange(terms, ("near", "chip", "core")).sum(0)
         place = lax.axis_index("chip") * 2 + core
         own_weight = lax.dynamic_slice_in_dim(doc_weight, place * own, own, 0)
         return scores * own_weight[:, None]

time: 137 us -> 132 us (0.964)
  blocking collectives: 79 us -> 63 us
  starting transfers between devices: 36.1 us -> 43.6 us
  waiting for transfers between devices: 13.3 us -> 16.9 us
    all_to_all x4 -> x3, blocking collectives: 79 us -> 63 us  [exchange(): return lax.all_to_all(pieces, axis, split_axis=0, concat_axis=0, tiled=True)]
    all_to_all x2, starting transfers between devices: 21.9 us -> 29.4 us  [exchange(): return lax.all_to_all(pieces, axis, split_axis=0, concat_axis=0, tiled=True)]
    all_to_all x2, waiting for transfers between devices: 10.9 us -> 14.4 us  [exchange(): return lax.all_to_all(pieces, axis, split_axis=0, concat_axis=0, tiled=True)]
where the time goes in v3:
time: 132 us
  blocking collectives  63 us (48%)
  starting transfers between devices  43.6 us (33%)
  waiting for transfers between devices  16.9 us (13%)
  local copies, waits for them, and re-layouts  4.98 us (4%)
  Pallas kernels  2.26 us (2%)
    all_to_all x3, blocking collectives, exchange(): return lax.all_to_all(pieces, axis, split_axis=0, concat_axis=0, tiled=True)  63 us
    all_to_all x2, starting transfers between devices, exchange(): return lax.all_to_all(pieces, axis, split_axis=0, concat_axis=0, tiled=True)  29.4 us
    all_to_all x2, waiting for transfers between devices, exchange(): return lax.all_to_all(pieces, axis, split_axis=0, concat_axis=0, tiled=True)  14.4 us
    ppermute x3, starting transfers between devices, on_device(): blocks.append(lax.ppermute(block, 'near', pairs) if s else block)  9.88 us
    ppermute x1, starting transfers between devices, on_device(): other = lax.ppermute(mine, 'core', swap)  4.31 us
  transfers between devices with their start and end apart: 6, of which 5 were waited for; matrix products, arithmetic and copies ran while one was open for 1% of the time, Pallas kernels for 1%

profile of v3, /device:TPU:1, one launch (start us, length us, event | category | flops | bytes accessed | tf_op | source)
XLA Modules:
  0.0 131.7 jit_solution(2381087233155331990)
XLA Ops:
  0.0 0.0 copy-start
  0.0 1.0 copy-done
  1.0 0.7 dynamic-slice_bitcast_fusion
  1.8 18.7 %all-to-all-start = ((f32[32,8,256]{2,1,0:T(8,128)}), f32[32,8,256]{2,1,0:T(8,128)S(1)}, u32[]{:S(2)}, u32[]{:S(2)}) async-start(f32[32,8,256]{2,1,0:T(8,128)} %dynamic-slice_bitcast_fusion), calls=%async_computation | async-start | bytes 524288 | tf_op jit(solution)/shard_map/all_to_all | solution.py:17
  20.4 0.8 constant_dynamic-slice_fusion
  21.3 5.5 %collective-permute-start.2 = (f32[32,256]{1,0:T(8,128)S(1)}, f32[32,256]{1,0:T(8,128)S(1)}, u32[]{:S(2)}, u32[]{:S(2)}) collective-permute-start(f32[32,256]{1,0:T(8,128)S(1)} %get-tuple-element.23), channel_id=1, source_target_pairs={{0,48},{16,32},{32,16},{48,0},{1,49},{17,33},{33,17},{49,1},{2,50}... | collective-permute-start | bytes 98312 | tf_op jit(solution)/shard_map/ppermute | solution.py:175
  26.8 2.2 %collective-permute-start = (f32[32,256]{1,0:T(8,128)S(1)}, f32[32,256]{1,0:T(8,128)S(1)}, u32[]{:S(2)}, u32[]{:S(2)}) collective-permute-start(f32[32,256]{1,0:T(8,128)S(1)} %get-tuple-element.24), channel_id=1, source_target_pairs={{0,16},{16,0},{32,48},{48,32},{1,17},{17,1},{33,49},{49,33},{2,18}... | collective-permute-start | bytes 98312 | tf_op jit(solution)/shard_map/ppermute | solution.py:175
  29.0 2.1 %collective-permute-start.1 = (f32[32,256]{1,0:T(8,128)S(1)}, f32[32,256]{1,0:T(8,128)S(1)}, u32[]{:S(2)}, u32[]{:S(2)}) collective-permute-start(f32[32,256]{1,0:T(8,128)S(1)} %get-tuple-element.26), channel_id=1, source_target_pairs={{0,32},{16,48},{32,0},{48,16},{1,33},{17,49},{33,1},{49,17},{2,34}... | collective-permute-start | bytes 98312 | tf_op jit(solution)/shard_map/ppermute | solution.py:175
  31.2 0.1 pad_add_fusion.place_ref
  31.3 0.0 copy-start.1
  31.3 1.6 %copy-done.1 = f32[512,1024]{1,0:T(8,128)S(1)} copy-done((f32[512,1024]{1,0:T(8,128)S(1)}, f32[512,1024]{1,0:T(8,128)}, u32[]{:S(2)}) %copy-start.1) | copy-done | bytes 2097176
  32.9 0.4 split_inverse.1
  33.3 0.7 collective-permute-done.2.refs_3_
  34.0 0.0 collective-permute-done.refs_1_
  34.0 0.5 collective-permute-done.1.refs_2_
  34.5 0.6 split_docs.1
  35.1 6.0 %all-to-all-done = f32[32,8,256]{2,1,0:T(8,128)S(1)} async-done(((f32[32,8,256]{2,1,0:T(8,128)}), f32[32,8,256]{2,1,0:T(8,128)S(1)}, u32[]{:S(2)}, u32[]{:S(2)}) %all-to-all-start) | async-done | bytes 262176 | tf_op jit(solution)/shard_map/all_to_all | solution.py:17
  41.2 4.3 %collective-permute-start.3 = (f32[256,256]{1,0:T(8,128)S(1)}, f32[256,256]{1,0:T(8,128)S(1)}, u32[]{:S(2)}, u32[]{:S(2)}) collective-permute-start(f32[256,256]{1,0:T(8,128)S(1)} %bitcast.15), channel_id=1, source_target_pairs={{0,1},{1,0},{2,3},{3,2},{4,5},{5,4},{6,7},{7,6},{8,9},{9,8},{10,11... | collective-permute-start | bytes 786440 | tf_op jit(solution)/shard_map/ppermute | solution.py:179
  45.5 1.1 collective-permute-done.3.other_ref
  46.6 1.0 mix_targets.1
  47.6 18.5 %all_to_all.25 = f32[4,256,256]{2,1,0:T(8,128)S(1)} all-to-all(f32[4,256,256]{2,1,0:T(8,128)S(1)} %mix_targets.1), channel_id=1, replica_groups=mesh['far'=8,'near'=4,'chip'=8,'core'=2] {'near'}, dimensions={0} | all-to-all | bytes 2097152 | tf_op jit(solution)/shard_map/all_to_all | solution.py:17
  66.1 0.0 copy-start.2
  66.1 0.1 reduce_sum.18
  66.1 21.2 %all_to_all.26.x_ref = f32[8,32,256]{2,1,0:T(8,128)S(1)} all-to-all(f32[8,32,256]{2,1,0:T(8,128)S(1)} %bitcast.17), channel_id=1, replica_groups=mesh['far'=8,'near'=4,'chip'=8,'core'=2] {'far'}, dimensions={0} | all-to-all | bytes 524288 | tf_op jit(solution)/shard_map/all_to_all | solution.py:17
  87.4 23.3 %all_to_all.27 = f32[8,32,256]{2,1,0:T(8,128)S(1)} all-to-all(f32[8,32,256]{2,1,0:T(8,128)S(1)} %sum_copies.1), channel_id=1, replica_groups=mesh['far'=8,'near'=4,'chip'=8,'core'=2] {'far'}, dimensions={0} | all-to-all | bytes 524288 | tf_op jit(solution)/shard_map/all_to_all | solution.py:17
  110.7 0.3 score_docs.1
  111.0 0.7 reshape.24
  111.7 10.7 %all-to-all-start.4 = ((f32[64,2,256]{2,1,0:T(2,128)}), f32[64,2,256]{2,1,0:T(2,128)S(1)}, u32[]{:S(2)}, u32[]{:S(2)}) async-start(f32[64,2,256]{2,1,0:T(2,128)} %reshape.24), calls=%async_computation.4 | async-start | bytes 262144 | tf_op jit(solution)/shard_map/all_to_all | solution.py:17
  122.5 0.0 copy-done.2
  122.5 0.1 dynamic_slice.24
  122.6 8.4 %all-to-all-done.4 = f32[64,2,256]{2,1,0:T(2,128)S(1)} async-done(((f32[64,2,256]{2,1,0:T(2,128)}), f32[64,2,256]{2,1,0:T(2,128)S(1)}, u32[]{:S(2)}, u32[]{:S(2)}) %all-to-all-start.4) | async-done | bytes 131104 | tf_op jit(solution)/shard_map/all_to_all | solution.py:17
  131.0 0.1 reduce_sum.19
  131.1 0.6 broadcast_multiply_fusion
  (1 shorter events, 0.0 us)
Async XLA Ops:
  0.0 1.0 copy-start
  1.8 39.4 %all-to-all-start = ((f32[32,8,256]{2,1,0:T(8,128)}), f32[32,8,256]{2,1,0:T(8,128)S(1)}, u32[]{:S(2)}, u32[]{:S(2)}) async-start(f32[32,8,256]{2,1,0:T(8,128)} %dynamic-slice_bitcast_fusion), calls=%async_computation | async-start | bytes 524288 | tf_op jit(solution)/shard_map/all_to_all | solution.py:17
  21.3 12.7 %collective-permute-start.2 = (f32[32,256]{1,0:T(8,128)S(1)}, f32[32,256]{1,0:T(8,128)S(1)}, u32[]{:S(2)}, u32[]{:S(2)}) collective-permute-start(f32[32,256]{1,0:T(8,128)S(1)} %get-tuple-element.23), channel_id=1, source_target_pairs={{0,48},{16,32},{32,16},{48,0},{1,49},{17,33},{33,17},{49,1},{2,50}... | collective-permute-start | bytes 98312 | tf_op jit(solution)/shard_map/ppermute | solution.py:175
  26.8 7.2 %collective-permute-start = (f32[32,256]{1,0:T(8,128)S(1)}, f32[32,256]{1,0:T(8,128)S(1)}, u32[]{:S(2)}, u32[]{:S(2)}) collective-permute-start(f32[32,256]{1,0:T(8,128)S(1)} %get-tuple-element.24), channel_id=1, source_target_pairs={{0,16},{16,0},{32,48},{48,32},{1,17},{17,1},{33,49},{49,33},{2,18}... | collective-permute-start | bytes 98312 | tf_op jit(solution)/shard_map/ppermute | solution.py:175
  29.0 5.5 %collective-permute-start.1 = (f32[32,256]{1,0:T(8,128)S(1)}, f32[32,256]{1,0:T(8,128)S(1)}, u32[]{:S(2)}, u32[]{:S(2)}) collective-permute-start(f32[32,256]{1,0:T(8,128)S(1)} %get-tuple-element.26), channel_id=1, source_target_pairs={{0,32},{16,48},{32,0},{48,16},{1,33},{17,49},{33,1},{49,17},{2,34}... | collective-permute-start | bytes 98312 | tf_op jit(solution)/shard_map/ppermute | solution.py:175
  31.3 1.6 %copy-start.1 = (f32[512,1024]{1,0:T(8,128)S(1)}, f32[512,1024]{1,0:T(8,128)}, u32[]{:S(2)}) copy-start(f32[512,1024]{1,0:T(8,128)} %k_ref.1) | copy-start | bytes 6291460
  41.2 5.5 %collective-permute-start.3 = (f32[256,256]{1,0:T(8,128)S(1)}, f32[256,256]{1,0:T(8,128)S(1)}, u32[]{:S(2)}, u32[]{:S(2)}) collective-permute-start(f32[256,256]{1,0:T(8,128)S(1)} %bitcast.15), channel_id=1, source_target_pairs={{0,1},{1,0},{2,3},{3,2},{4,5},{5,4},{6,7},{7,6},{8,9},{9,8},{10,11... | collective-permute-start | bytes 786440 | tf_op jit(solution)/shard_map/ppermute | solution.py:179
  66.1 56.4 %copy-start.2 = (f32[32]{0:T(128)S(1)}, f32[32]{0:T(128)}, u32[]{:S(2)}) copy-start(f32[32]{0:T(128)} %param.7) | copy-start | bytes 388
  111.7 19.2 %all-to-all-start.4 = ((f32[64,2,256]{2,1,0:T(2,128)}), f32[64,2,256]{2,1,0:T(2,128)S(1)}, u32[]{:S(2)}, u32[]{:S(2)}) async-start(f32[64,2,256]{2,1,0:T(2,128)} %reshape.24), calls=%async_computation.4 | async-start | bytes 262144 | tf_op jit(solution)/shard_map/all_to_all | solution.py:17

commit v4 on v3

--- a/solution.py
+++ b/solution.py
@@ -56,32 +56,31 @@
     )(kernel_inv)
 
 
-def mix_targets(core, mine, other, k_hi, k_lo):
-    all_t, half = mine.shape
+def mix_targets(both, k_hi, k_lo):
+    cores, all_t, half = both.shape
     n_j = k_hi.shape[1]
     sub = n_j // NEAR
 
-    def body(core_ref, mine_ref, other_ref, hi_ref, lo_ref, out_ref):
-        place = core_ref[0]
-        sides = [(split(mine_ref[...]), place), (split(other_ref[...]), 1 - place)]
+    def body(both_ref, hi_ref, lo_ref, out_ref):
+        sides = [split(both_ref[s]) for s in range(cores)]
         for a in range(NEAR):
             cut = slice(a * sub, (a + 1) * sub)
             total = None
-            for t, at in sides:
-                rows = pl.ds(pl.multiple_of(at * half, half), half)
+            for s, t in enumerate(sides):
+                rows = slice(s * half, (s + 1) * half)
                 part = dot3(t, (hi_ref[rows, cut], lo_ref[rows, cut]), 1, 0)
                 total = part if total is None else total + part
             out_ref[a] = total
 
     return pl.pallas_call(
         body,
-        in_specs=[SMEM, VMEM, VMEM, VMEM, VMEM],
+        in_specs=[VMEM, VMEM, VMEM],
         out_specs=VMEM,
         out_shape=jax.ShapeDtypeStruct((NEAR, all_t, sub), jnp.float32),
         compiler_params=PARAMS,
-        cost_estimate=cost(6 * all_t * 2 * half * n_j, 4 * 2**20),
+        cost_estimate=cost(6 * all_t * cores * half * n_j, 4 * 2**20),
         name="mix_targets",
-    )(core, mine, other, k_hi, k_lo)
+    )(both, k_hi, k_lo)
 
 
 def split_docs(place, blocks):
@@ -151,7 +150,6 @@
     names = ("far", "near", "chip", "core")
     fine = Mesh(mesh.devices.reshape(far, NEAR, chips, 2), names)
     row, col = ("far", "near"), ("chip", "core")
-    swap = [(0, 1), (1, 0)]
 
     def on_device(doc_feats, kernel_inv, target_feats, doc_weight):
         core = lax.axis_index("core")
@@ -176,8 +174,8 @@
         d_hi, d_lo = split_docs(place, blocks)
         mine, k_hi, k_lo, d_hi, d_lo = lax.optimization_barrier((mine, k_hi, k_lo, d_hi, d_lo))
 
-        other = lax.ppermute(mine, "core", swap)
-        mixed = mix_targets(core.reshape(1), mine, other, k_hi, k_lo)
+        both = lax.all_gather(mine, "core")
+        mixed = mix_targets(both, k_hi, k_lo)
         mixed = exchange(mixed, "near").sum(0)
         mixed = exchange(mixed.reshape(far, all_t // far, sub), "far")
         mixed = exchange(sum_copies(mixed), "far").reshape(all_t, sub)

time: 132 us -> 131 us (level)
  starting transfers between devices: 43.6 us -> 39.3 us
  blocking collectives: 63 us -> 67.2 us
    ppermute x1 -> x0, starting transfers between devices: 4.31 us -> none  [on_device(): other = lax.ppermute(mine, 'core', swap)]
    all_gather x0 -> x1, blocking collectives: none -> 4.21 us  [on_device(): both = lax.all_gather(mine, 'core')]
  transfers between devices with their start and end apart: 6 -> 5, of which waited for: 5 -> 4; matrix products, arithmetic and copies ran while one was open for 1% -> 1% of each run, Pallas kernels for 1% -> 1%
where the time goes in v4:
time: 131 us
  blocking collectives  67.2 us (51%)
  starting transfers between devices  39.3 us (30%)
  waiting for transfers between devices  15.7 us (12%)
  local copies, waits for them, and re-layouts  4.99 us (4%)
  Pallas kernels  2.25 us (2%)
    all_to_all x3, blocking collectives, exchange(): return lax.all_to_all(pieces, axis, split_axis=0, concat_axis=0, tiled=True)  63 us
    all_to_all x2, starting transfers between devices, exchange(): return lax.all_to_all(pieces, axis, split_axis=0, concat_axis=0, tiled=True)  29.5 us
    all_to_all x2, waiting for transfers between devices, exchange(): return lax.all_to_all(pieces, axis, split_axis=0, concat_axis=0, tiled=True)  14.4 us
    ppermute x3, starting transfers between devices, on_device(): blocks.append(lax.ppermute(block, 'near', pairs) if s else block)  9.88 us
    all_gather x1, blocking collectives, on_device(): both = lax.all_gather(mine, 'core')  4.21 us
    unnamed x6, local copies, waits for them, and re-layouts  2.64 us
  transfers between devices with their start and end apart: 5, of which 4 were waited for; matrix products, arithmetic and copies ran while one was open for 1% of the time, Pallas kernels for 1%

profile of v4, /device:TPU:1, one launch (start us, length us, event | category | flops | bytes accessed | tf_op | source)
XLA Modules:
  0.0 130.5 jit_solution(10261395758181127580)
XLA Ops:
  0.0 0.0 copy-start
  0.0 1.0 copy-done
  1.0 0.7 dynamic-slice_bitcast_fusion
  1.8 18.7 %all-to-all-start = ((f32[32,8,256]{2,1,0:T(8,128)}), f32[32,8,256]{2,1,0:T(8,128)S(1)}, u32[]{:S(2)}, u32[]{:S(2)}) async-start(f32[32,8,256]{2,1,0:T(8,128)} %dynamic-slice_bitcast_fusion), calls=%async_computation | async-start | bytes 524288 | tf_op jit(solution)/shard_map/all_to_all | solution.py:17
  20.5 0.8 constant_dynamic-slice_fusion
  21.3 5.5 %collective-permute-start.2 = (f32[32,256]{1,0:T(8,128)S(1)}, f32[32,256]{1,0:T(8,128)S(1)}, u32[]{:S(2)}, u32[]{:S(2)}) collective-permute-start(f32[32,256]{1,0:T(8,128)S(1)} %get-tuple-element.23), channel_id=1, source_target_pairs={{0,48},{16,32},{32,16},{48,0},{1,49},{17,33},{33,17},{49,1},{2,50}... | collective-permute-start | bytes 98312 | tf_op jit(solution)/shard_map/ppermute | solution.py:173
  26.8 2.2 %collective-permute-start = (f32[32,256]{1,0:T(8,128)S(1)}, f32[32,256]{1,0:T(8,128)S(1)}, u32[]{:S(2)}, u32[]{:S(2)}) collective-permute-start(f32[32,256]{1,0:T(8,128)S(1)} %get-tuple-element.24), channel_id=1, source_target_pairs={{0,16},{16,0},{32,48},{48,32},{1,17},{17,1},{33,49},{49,33},{2,18}... | collective-permute-start | bytes 98312 | tf_op jit(solution)/shard_map/ppermute | solution.py:173
  29.0 2.1 %collective-permute-start.1 = (f32[32,256]{1,0:T(8,128)S(1)}, f32[32,256]{1,0:T(8,128)S(1)}, u32[]{:S(2)}, u32[]{:S(2)}) collective-permute-start(f32[32,256]{1,0:T(8,128)S(1)} %get-tuple-element.26), channel_id=1, source_target_pairs={{0,32},{16,48},{32,0},{48,16},{1,33},{17,49},{33,1},{49,17},{2,34}... | collective-permute-start | bytes 98312 | tf_op jit(solution)/shard_map/ppermute | solution.py:173
  31.2 0.1 pad_add_fusion.place_ref
  31.3 0.0 copy-start.1
  31.3 1.6 %copy-done.1 = f32[512,1024]{1,0:T(8,128)S(1)} copy-done((f32[512,1024]{1,0:T(8,128)S(1)}, f32[512,1024]{1,0:T(8,128)}, u32[]{:S(2)}) %copy-start.1) | copy-done | bytes 2097176
  32.9 0.4 split_inverse.1
  33.3 0.7 collective-permute-done.2.refs_3_
  34.0 0.0 collective-permute-done.refs_1_
  34.0 0.5 collective-permute-done.1.refs_2_
  34.6 0.6 split_docs.1
  35.1 6.0 %all-to-all-done = f32[32,8,256]{2,1,0:T(8,128)S(1)} async-done(((f32[32,8,256]{2,1,0:T(8,128)}), f32[32,8,256]{2,1,0:T(8,128)S(1)}, u32[]{:S(2)}, u32[]{:S(2)}) %all-to-all-start) | async-done | bytes 262176 | tf_op jit(solution)/shard_map/all_to_all | solution.py:17
  41.2 4.2 %all-gather = f32[512,256]{1,0:T(8,128)S(1)} all-gather(f32[256,256]{1,0:T(8,128)S(1)} %bitcast.16), channel_id=2, replica_groups=mesh['far'=8,'near'=4,'chip'=8,'core'=2] {'core'}, dimensions={0}, use_global_device_ids=true | all-gather | bytes 786432 | tf_op jit(solution)/shard_map/all_gather | solution.py:177
  45.4 1.0 mix_targets.1
  46.3 18.5 %all_to_all.25 = f32[4,256,256]{2,1,0:T(8,128)S(1)} all-to-all(f32[4,256,256]{2,1,0:T(8,128)S(1)} %mix_targets.1), channel_id=1, replica_groups=mesh['far'=8,'near'=4,'chip'=8,'core'=2] {'near'}, dimensions={0} | all-to-all | bytes 2097152 | tf_op jit(solution)/shard_map/all_to_all | solution.py:17
  64.8 0.0 copy-start.2
  64.8 0.1 reduce_sum.18
  64.9 21.2 %all_to_all.26.x_ref = f32[8,32,256]{2,1,0:T(8,128)S(1)} all-to-all(f32[8,32,256]{2,1,0:T(8,128)S(1)} %bitcast.17), channel_id=1, replica_groups=mesh['far'=8,'near'=4,'chip'=8,'core'=2] {'far'}, dimensions={0} | all-to-all | bytes 524288 | tf_op jit(solution)/shard_map/all_to_all | solution.py:17
  86.1 23.3 %all_to_all.27 = f32[8,32,256]{2,1,0:T(8,128)S(1)} all-to-all(f32[8,32,256]{2,1,0:T(8,128)S(1)} %sum_copies.1), channel_id=1, replica_groups=mesh['far'=8,'near'=4,'chip'=8,'core'=2] {'far'}, dimensions={0} | all-to-all | bytes 524288 | tf_op jit(solution)/shard_map/all_to_all | solution.py:17
  109.5 0.3 score_docs.1
  109.7 0.7 reshape.20
  110.5 10.8 %all-to-all-start.4 = ((f32[64,2,256]{2,1,0:T(2,128)}), f32[64,2,256]{2,1,0:T(2,128)S(1)}, u32[]{:S(2)}, u32[]{:S(2)}) async-start(f32[64,2,256]{2,1,0:T(2,128)} %reshape.20), calls=%async_computation.4 | async-start | bytes 262144 | tf_op jit(solution)/shard_map/all_to_all | solution.py:17
  121.3 0.0 copy-done.2
  121.3 0.1 dynamic_slice.24
  121.4 8.4 %all-to-all-done.4 = f32[64,2,256]{2,1,0:T(2,128)S(1)} async-done(((f32[64,2,256]{2,1,0:T(2,128)}), f32[64,2,256]{2,1,0:T(2,128)S(1)}, u32[]{:S(2)}, u32[]{:S(2)}) %all-to-all-start.4) | async-done | bytes 131104 | tf_op jit(solution)/shard_map/all_to_all | solution.py:17
  129.8 0.1 reduce_sum.19
  129.9 0.6 broadcast_multiply_fusion
  (1 shorter events, 0.0 us)
Async XLA Ops:
  0.0 1.0 copy-start
  1.8 39.4 %all-to-all-start = ((f32[32,8,256]{2,1,0:T(8,128)}), f32[32,8,256]{2,1,0:T(8,128)S(1)}, u32[]{:S(2)}, u32[]{:S(2)}) async-start(f32[32,8,256]{2,1,0:T(8,128)} %dynamic-slice_bitcast_fusion), calls=%async_computation | async-start | bytes 524288 | tf_op jit(solution)/shard_map/all_to_all | solution.py:17
  21.3 12.7 %collective-permute-start.2 = (f32[32,256]{1,0:T(8,128)S(1)}, f32[32,256]{1,0:T(8,128)S(1)}, u32[]{:S(2)}, u32[]{:S(2)}) collective-permute-start(f32[32,256]{1,0:T(8,128)S(1)} %get-tuple-element.23), channel_id=1, source_target_pairs={{0,48},{16,32},{32,16},{48,0},{1,49},{17,33},{33,17},{49,1},{2,50}... | collective-permute-start | bytes 98312 | tf_op jit(solution)/shard_map/ppermute | solution.py:173
  26.8 7.2 %collective-permute-start = (f32[32,256]{1,0:T(8,128)S(1)}, f32[32,256]{1,0:T(8,128)S(1)}, u32[]{:S(2)}, u32[]{:S(2)}) collective-permute-start(f32[32,256]{1,0:T(8,128)S(1)} %get-tuple-element.24), channel_id=1, source_target_pairs={{0,16},{16,0},{32,48},{48,32},{1,17},{17,1},{33,49},{49,33},{2,18}... | collective-permute-start | bytes 98312 | tf_op jit(solution)/shard_map/ppermute | solution.py:173
  29.0 5.5 %collective-permute-start.1 = (f32[32,256]{1,0:T(8,128)S(1)}, f32[32,256]{1,0:T(8,128)S(1)}, u32[]{:S(2)}, u32[]{:S(2)}) collective-permute-start(f32[32,256]{1,0:T(8,128)S(1)} %get-tuple-element.26), channel_id=1, source_target_pairs={{0,32},{16,48},{32,0},{48,16},{1,33},{17,49},{33,1},{49,17},{2,34}... | collective-permute-start | bytes 98312 | tf_op jit(solution)/shard_map/ppermute | solution.py:173
  31.3 1.6 %copy-start.1 = (f32[512,1024]{1,0:T(8,128)S(1)}, f32[512,1024]{1,0:T(8,128)}, u32[]{:S(2)}) copy-start(f32[512,1024]{1,0:T(8,128)} %k_ref.1) | copy-start | bytes 6291460
  64.8 56.5 %copy-start.2 = (f32[32]{0:T(128)S(1)}, f32[32]{0:T(128)}, u32[]{:S(2)}) copy-start(f32[32]{0:T(128)} %param.7) | copy-start | bytes 388
  110.5 19.3 %all-to-all-start.4 = ((f32[64,2,256]{2,1,0:T(2,128)}), f32[64,2,256]{2,1,0:T(2,128)S(1)}, u32[]{:S(2)}, u32[]{:S(2)}) async-start(f32[64,2,256]{2,1,0:T(2,128)} %reshape.20), calls=%async_computation.4 | async-start | bytes 262144 | tf_op jit(solution)/shard_map/all_to_all | solution.py:17
